TPU v7x, 1024 devices: a whole 4x4x32 slice. The times are simulated.
1024 devices in a mesh: section: 8 (over z_lo), expert: 16 (over y, x), dp: 8 (over z_hi, core).
Axes of the slice: x: 4, y: 4, z: 32 (z_hi: 4, z_lo: 8; z = z_hi * 8 + z_lo), core: 2. Of those that a mesh axis runs over, the one named last changes fastest.
Arguments:
- section_out: bfloat16 [8, 640, 3072], P('section', 'expert'), may hold values from -6 to 6
- routes_fwd: int32 [8, 640, 4], P('section', 'expert'), may hold values from 0 to 15, all different within a row; in each aligned block of 40 rows (0 to 39, 40 to 79, ..., all dimensions but the last counted through in order) at most 13 rows name the same one
- gate_weight: bfloat16 [16, 3072, 5376], P('expert', None, 'dp'), may hold values from -0.109375 to 0.109375
- up_weight: bfloat16 [16, 3072, 5376], P('expert', None, 'dp'), may hold values from -0.109375 to 0.109375
- routes_bwd: int32 [8, 640, 4], P('section', 'expert'), may hold values from 0 to 15, all different within a row; in each aligned block of 40 rows (0 to 39, 40 to 79, ..., all dimensions but the last counted through in order) at most 13 rows name the same one
- saved_gate: bfloat16 [8, 16, 208, 5376], P('section', 'expert', None, 'dp'), may hold values from -8 to 8
- saved_up: bfloat16 [8, 16, 208, 5376], P('section', 'expert', None, 'dp'), may hold values from -6 to 6
- grad_hidden: bfloat16 [8, 16, 208, 5376], P('section', 'expert', None, 'dp'), may hold values from -6 to 6
Outputs:
- hidden_out: bfloat16 [8, 16, 208, 5376], P('section', 'expert', None, 'dp')
- grad_input: bfloat16 [8, 640, 3072], P('section', 'expert', 'dp')
Inputs may be any that keep to these rules, and one draw needn't show every extreme that they name: `routes_fwd`: in each aligned block of 40 rows (one token group) of a section, no expert is named by more than 13 rows, a bound that some block reaches. `routes_bwd`: in each aligned block of 40 rows (one token group) of a section, no expert is named by more than 13 rows, a bound that some block reaches.
All inputs are finite; a program needn't handle non-finite values.
Results may differ from a plain program's by a relative error of at most 0.02.
Values may be sent and summed in bfloat16 or wider, within the bound.
A program may use at most 32 MiB of HBM per device.

v0:
```python
import jax
import jax.numpy as jnp
from jax import lax
from jax.sharding import PartitionSpec as P


def from_behind(block, axis, distance):
    devices = range(lax.axis_size(axis))
    route = [((i - distance) % len(devices), i) for i in devices]
    return lax.ppermute(block, axis, route)


def slot_table(routes_group, experts, capacity):
    tokens_here = routes_group.shape[0]
    chosen = routes_group.reshape(-1)
    onehot = (chosen[:, None] == jnp.arange(experts, dtype=jnp.int32)[None, :]).astype(jnp.int32)
    earlier = jnp.cumsum(onehot, axis=0) - onehot
    position = jnp.sum(earlier * onehot, axis=1)
    slot_index = (chosen * capacity + position).reshape(tokens_here, -1)
    targets = jnp.arange(experts * capacity, dtype=jnp.int32)
    matches = jnp.sum((slot_index[None, :, :] == targets[:, None, None]).astype(jnp.int32), axis=2)
    return matches.astype(jnp.bfloat16)


def per_device(
    section_out, routes_fwd, gate_weight, up_weight, routes_bwd, saved_gate, saved_up, grad_hidden
):
    experts = lax.axis_size("expert")
    shards = lax.axis_size("dp")
    slots = saved_gate.shape[2]
    capacity = slots // experts
    width = section_out.shape[2]
    width_dev = width // shards
    lane_width = min(128, width_dev)
    blocks_dev = width_dev // lane_width
    hidden_dev = gate_weight.shape[2]
    gate_w = gate_weight[0]
    up_w = up_weight[0]
    fwd_map = slot_table(routes_fwd[0], experts, capacity)
    incoming = from_behind(section_out[0], "section", 1)
    outgoing = jnp.dot(fwd_map, incoming, preferred_element_type=jnp.float32).astype(jnp.bfloat16)
    received = lax.all_to_all(
        outgoing.reshape(experts, capacity, width),
        "expert",
        split_axis=0,
        concat_axis=0,
        tiled=True,
    )
    flat_rows = received.reshape(-1, width)
    gate_pre = jnp.dot(flat_rows, gate_w, preferred_element_type=jnp.float32)
    up_pre = jnp.dot(flat_rows, up_w, preferred_element_type=jnp.float32)
    result = (jax.nn.silu(gate_pre) * up_pre).astype(jnp.bfloat16)
    hidden = result.reshape(received.shape[0], received.shape[1], hidden_dev)
    hidden = hidden.reshape(slots, hidden_dev)
    gate_saved = saved_gate[0, 0].astype(jnp.float32)
    up_saved = saved_up[0, 0].astype(jnp.float32)
    cotangent = grad_hidden[0, 0].astype(jnp.float32)
    sigmoid_gate = jax.nn.sigmoid(gate_saved)
    grad_up = (cotangent * gate_saved * sigmoid_gate).astype(jnp.bfloat16)
    grad_gate = (
        cotangent * up_saved * sigmoid_gate * (1.0 + gate_saved * (1.0 - sigmoid_gate))
    ).astype(jnp.bfloat16)
    dims = (((1,), (1,)), ((), ()))
    first = lax.dot_general(grad_gate, gate_w, dims, preferred_element_type=jnp.float32)
    second = lax.dot_general(grad_up, up_w, dims, preferred_element_type=jnp.float32)
    total = (first + second).reshape(slots, blocks_dev * lax.axis_size("dp"), lane_width)
    summed = lax.psum_scatter(
        total.transpose(1, 0, 2).astype(jnp.bfloat16), "dp", scatter_dimension=0, tiled=True
    )
    sending = summed.reshape(blocks_dev, experts, capacity, lane_width)
    returned = lax.all_to_all(sending, "expert", split_axis=1, concat_axis=1, tiled=True).reshape(
        blocks_dev, slots, lane_width
    )
    bwd_map = slot_table(routes_bwd[0], experts, capacity)
    token_grads = jnp.einsum("st,csl->tcl", bwd_map, returned, preferred_element_type=jnp.float32)
    grad_input = token_grads.reshape(token_grads.shape[0], width_dev).astype(jnp.bfloat16)[None]
    return (hidden.reshape(1, 1, slots, hidden_dev), grad_input)


def solution(mesh):
    in_specs = (
        P("section", "expert", None),
        P("section", "expert", None),
        P("expert", None, "dp"),
        P("expert", None, "dp"),
        P("section", "expert", None),
        P("section", "expert", None, "dp"),
        P("section", "expert", None, "dp"),
        P("section", "expert", None, "dp"),
    )
    out_specs = (P("section", "expert", None, "dp"), P("section", "expert", "dp"))
    return jax.shard_map(
        per_device, mesh=mesh, in_specs=in_specs, out_specs=out_specs, check_vma=False
    )
```

profile of v0, /device:TPU:2, one launch (start us, length us, event | category | flops | bytes accessed | tf_op | source)
XLA Modules:
  0.0 151.8 jit_solution(9934005780648645561)
XLA Ops:
  7.3 4.1 %collective-permute-start = (bf16[40,3072]{1,0:T(8,128)(2,1)}, bf16[40,3072]{1,0:T(8,128)(2,1)S(1)}, u32[]{:S(2)}, u32[]{:S(2)}) collective-permute-start(bf16[40,3072]{1,0:T(8,128)(2,1)} %bitcast.78), channel_id=1, source_target_pairs={{896,0},{0,128},{128,256},{256,384},{384,512},{512,640},{640,768},... | collective-permute-start | bytes 737288 | tf_op jit(solution)/shard_map/ppermute | solution.py:10
  11.3 3.6 %fusion = f32[208,3072]{1,0:T(8,128)S(1)} fusion(bf16[1,3072,672]{1,2,0:T(8,128)(2,1)} %param.11, bf16[1,1,208,672]{3,2,1,0:T(8,128)(2,1)} %param.13, bf16[1,1,208,672]{3,2,1,0:T(8,128)(2,1)} %param.15), kind=kOutput, calls=%fused_computation | convolution fusion | flops 859901952 | bytes 7243776 | tf_op jit(solution)/shard_map/dot_general | solution.py:65
  15.0 1.4 fusion.14
  16.4 1.3 copy.99
  17.9 0.6 reduce-window.14
  18.5 0.2 slice_reduce_fusion.1
  19.1 0.1 convert_reduce_fusion.1
  19.2 7.7 %collective-permute-done = bf16[40,3072]{1,0:T(8,128)(2,1)S(1)} collective-permute-done((bf16[40,3072]{1,0:T(8,128)(2,1)}, bf16[40,3072]{1,0:T(8,128)(2,1)S(1)}, u32[]{:S(2)}, u32[]{:S(2)}) %collective-permute-start) | collective-permute-done | bytes 245792 | tf_op jit(solution)/shard_map/ppermute | solution.py:10
  26.8 0.5 convolution_convert_fusion
  27.4 1.4 reshape.50
  28.8 12.3 %all-to-all-start = ((bf16[16,13,3072]{2,1,0:T(8,128)(2,1)}), bf16[16,13,3072]{2,1,0:T(8,128)(2,1)S(1)}, u32[]{:S(2)}, u32[]{:S(2)}) async-start(bf16[16,13,3072]{2,1,0:T(8,128)(2,1)} %reshape.50), calls=%async_computation | async-start | bytes 3145728 | tf_op jit(solution)/shard_map/all_to_all | solution.py:42
  41.3 0.6 reduce-window.16
  41.8 0.2 slice_reduce_fusion
  42.5 15.4 %all-to-all-done = bf16[16,13,3072]{2,1,0:T(8,128)(2,1)S(1)} async-done(((bf16[16,13,3072]{2,1,0:T(8,128)(2,1)}), bf16[16,13,3072]{2,1,0:T(8,128)(2,1)S(1)}, u32[]{:S(2)}, u32[]{:S(2)}) %all-to-all-start) | async-done | bytes 1277984 | tf_op jit(solution)/shard_map/all_to_all | solution.py:42
  57.9 0.5 reshape.51
  58.4 3.6 %fusion.6 = f32[208,672]{1,0:T(8,128)S(1)} fusion(bf16[208,3072]{1,0:T(8,128)(2,1)S(1)} %reshape.51, bf16[1,3072,672]{1,2,0:T(8,128)(2,1)} %param.10), kind=kOutput, calls=%fused_computation.6 | convolution fusion | flops 858783744 | bytes 5965824 | tf_op jit(solution)/shard_map/dot_general | solution.py:50
  62.0 65.4 %reduce-scatter.2.cloned.1.call-done = bf16[3,208,128]{2,1,0:T(8,128)(2,1)} async-done(((bf16[24,208,128]{2,1,0:T(8,128)(2,1)}), bf16[3,208,128]{2,1,0:T(8,128)(2,1)}) %reduce-scatter.2.cloned.1.call-update) | async-done | bytes 159760 | tf_op jit(solution)/shard_map/reduce_scatter | solution.py:67
  127.4 1.0 reshape.54
  128.4 0.7 copy.86
  129.1 7.9 %all-to-all-start.1 = ((bf16[3,16,13,128]{3,2,0,1:T(8,128)(2,1)}), bf16[3,16,13,128]{3,2,0,1:T(8,128)(2,1)S(1)}, u32[]{:S(2)}, u32[]{:S(2)}) async-start(bf16[3,16,13,128]{3,2,0,1:T(8,128)(2,1)} %copy.86), calls=%async_computation.2 | async-start | bytes 393216 | tf_op jit(solution)/shard_map/all_to_all | solution.py:71
  136.9 4.4 %fusion.23 = bf16[1,1,208,672]{3,2,1,0:T(8,128)(2,1)} fusion(bf16[208,3072]{1,0:T(8,128)(2,1)S(1)} %reshape.51, bf16[1,3072,672]{1,2,0:T(8,128)(2,1)} %param.11, f32[208,672]{1,0:T(8,128)S(1)} %fusion.6), kind=kOutput, calls=%fused_computation.15 | convolution fusion | flops 859622400 | bytes 6245376 | tf_op jit(solution)/shard_map/dot_general | solution.py:51
  141.3 2.6 %all-to-all-done.1 = bf16[3,16,13,128]{3,2,0,1:T(8,128)(2,1)S(1)} async-done(((bf16[3,16,13,128]{3,2,0,1:T(8,128)(2,1)}), bf16[3,16,13,128]{3,2,0,1:T(8,128)(2,1)S(1)}, u32[]{:S(2)}, u32[]{:S(2)}) %all-to-all-start.1) | async-done | bytes 159776 | tf_op jit(solution)/shard_map/all_to_all | solution.py:71
  144.0 0.1 copy.88
  144.2 0.8 fusion.26
  (39 shorter events, 1.3 us)
Async XLA Ops:
  7.2 120.2 %reduce-scatter.2.cloned.1.call-start = ((), (), s32[]{:S(2)}) async-start(), calls=%async_computation.3 | async-start | bytes 1437696 | tf_op jit(solution)/shard_map/reduce_scatter | solution.py:67
  7.2 7.7 %copy-start.2 = (bf16[1,3072,672]{1,2,0:T(8,128)(2,1)S(1)}, bf16[1,3072,672]{1,2,0:T(8,128)(2,1)}, u32[]{:S(2)}) copy-start(bf16[1,3072,672]{1,2,0:T(8,128)(2,1)} %param.10) | copy-start | bytes 12386308
  7.2 7.7 %copy-start.3 = (bf16[1,1,208,672]{3,2,1,0:T(8,128)(2,1)S(1)}, bf16[1,1,208,672]{3,2,1,0:T(8,128)(2,1)}, u32[]{:S(2)}) copy-start(bf16[1,1,208,672]{3,2,1,0:T(8,128)(2,1)} %param.13) | copy-start | bytes 838660
  7.2 7.7 %copy-start.4 = (bf16[1,1,208,672]{3,2,1,0:T(8,128)(2,1)S(1)}, bf16[1,1,208,672]{3,2,1,0:T(8,128)(2,1)}, u32[]{:S(2)}) copy-start(bf16[1,1,208,672]{3,2,1,0:T(8,128)(2,1)} %param.15) | copy-start | bytes 838660
  7.2 7.7 %copy-start.5 = (bf16[1,1,208,672]{3,2,1,0:T(8,128)(2,1)S(1)}, bf16[1,1,208,672]{3,2,1,0:T(8,128)(2,1)}, u32[]{:S(2)}) copy-start(bf16[1,1,208,672]{3,2,1,0:T(8,128)(2,1)} %param.14) | copy-start | bytes 838660
  7.3 19.6 %collective-permute-start = (bf16[40,3072]{1,0:T(8,128)(2,1)}, bf16[40,3072]{1,0:T(8,128)(2,1)S(1)}, u32[]{:S(2)}, u32[]{:S(2)}) collective-permute-start(bf16[40,3072]{1,0:T(8,128)(2,1)} %bitcast.78), channel_id=1, source_target_pairs={{896,0},{0,128},{128,256},{256,384},{384,512},{512,640},{640,768},... | collective-permute-start | bytes 737288 | tf_op jit(solution)/shard_map/ppermute | solution.py:10
  16.4 1.3 copy-start
  27.4 13.7 %copy-start.1 = (s32[1,40,4]{1,2,0:T(4,128)S(1)}, s32[1,40,4]{1,2,0:T(4,128)}, u32[]{:S(2)}) copy-start(s32[1,40,4]{1,2,0:T(4,128)} %param.12) | copy-start | bytes 1924
  28.8 29.1 %all-to-all-start = ((bf16[16,13,3072]{2,1,0:T(8,128)(2,1)}), bf16[16,13,3072]{2,1,0:T(8,128)(2,1)S(1)}, u32[]{:S(2)}, u32[]{:S(2)}) async-start(bf16[16,13,3072]{2,1,0:T(8,128)(2,1)} %reshape.50), calls=%async_computation | async-start | bytes 3145728 | tf_op jit(solution)/shard_map/all_to_all | solution.py:42
  129.1 14.8 %all-to-all-start.1 = ((bf16[3,16,13,128]{3,2,0,1:T(8,128)(2,1)}), bf16[3,16,13,128]{3,2,0,1:T(8,128)(2,1)S(1)}, u32[]{:S(2)}, u32[]{:S(2)}) async-start(bf16[3,16,13,128]{3,2,0,1:T(8,128)(2,1)} %copy.86), calls=%async_computation.2 | async-start | bytes 393216 | tf_op jit(solution)/shard_map/all_to_all | solution.py:71
Sparse Core Ops, SparseCore 0:
  17.8 109.5 reduce-scatter.1
where the time goes:
time: 152 us
  waiting for transfers between devices  91.1 us (60%)
  starting transfers between devices  24.3 us (16%)
  matrix products  14.3 us (9%)
  between operations  14.3 us (9%)
  local copies, waits for them, and re-layouts  6.18 us (4%)
  other arithmetic  1.71 us (1%)
    reduce_scatter x1, waiting for transfers between devices, per_device(): lax.psum_scatter(total.transpose(1, 0, 2).astype(jnp.bfloat16), 'dp', sca...  65.4 us
    all_to_all x1, waiting for transfers between devices, per_device(): lax.all_to_all(outgoing.reshape(experts, capacity, width), 'expert', spli...  15.4 us
    all_to_all x1, starting transfers between devices, per_device(): lax.all_to_all(outgoing.reshape(experts, capacity, width), 'expert', spli...  12.3 us
    all_to_all x1, starting transfers between devices, per_device(): lax.all_to_all(sending, 'expert', split_axis=1, concat_axis=1, tiled=True)  7.87 us
    ppermute x1, waiting for transfers between devices, from_behind(): return lax.ppermute(block, axis, route)  7.66 us
    dot_general x1, matrix products, per_device(): up_pre = jnp.dot(flat_rows, up_w, preferred_element_type=jnp.float32)  4.36 us
    ppermute x1, starting transfers between devices, from_behind(): return lax.ppermute(block, axis, route)  4.09 us
    dot_general x1, matrix products, per_device(): gate_pre = jnp.dot(flat_rows, gate_w, preferred_element_type=jnp.float32)  3.63 us
  transfers between devices with their start and end apart: 4, of which 4 were waited for; matrix products, arithmetic and copies ran while one was open for 13% of the time, Pallas kernels for 0%

commit v1 on v0

v1 whole, which is shorter than its diff:
```python
import jax
import jax.numpy as jnp
from jax import lax
from jax.experimental import pallas as pl
from jax.experimental.pallas import tpu as pltpu
from jax.sharding import PartitionSpec as P

MESH = pl.DeviceIdType.MESH
F32, BF16 = jnp.float32, jnp.bfloat16

TOK = 40
TOKP = 48
CAP = 13
CAPP = 16
EXPERTS = 16
ROWS = EXPERTS * CAP
ROWSP = EXPERTS * CAPP
D = 3072
HALF = D // 2
BLOCK = D // 8
HI = 4
PIECES = 3
WIDE = HALF // PIECES
FAR_FIRST = (2, 1, 3, 0)


def dot(a, b):
    return jnp.dot(a, b, preferred_element_type=F32)


def dot_t(a, b):
    return lax.dot_general(a, b, (((1,), (1,)), ((), ())), preferred_element_type=F32)


def iota(shape, dim):
    return lax.broadcasted_iota(jnp.int32, shape, dim)


def positions(routes):
    e = iota((EXPERTS, TOK), 0)
    picked = jnp.zeros((EXPERTS, TOK), F32)
    for k in range(routes.shape[0]):
        picked = picked + (routes[k : k + 1, :] == e).astype(F32)
    picked = picked.astype(BF16)
    row, column = iota((TOK, TOKP), 0), iota((TOK, TOKP), 1)
    earlier = dot(picked, (row < column).astype(F32).astype(BF16))
    here = dot(picked, (row == column).astype(F32).astype(BF16))
    return jnp.where(here > 0.5, earlier, 99.0).astype(BF16)


def padding(shape, slot_dim):
    slot, row = iota(shape, slot_dim), iota(shape, 1 - slot_dim)
    return (slot // CAP * CAPP + slot % CAP == row).astype(F32).astype(BF16)


def kernel(
    sec, rf, gw, uw, rb, sg, su, gh,
    hidden_ref, grad_ref,
    secv, rfv, rbv, gwv, uwv, sgv, suv, ghv,
    tsend, trecv, pbuf, xrecv, asend, arecv, zsend, zrecv, fsend, frecv, foth,
    small_sem, load_sem, w_sem, ts, tr, xs, xr, as_, ar, zs, zr, fs, fr, gs, gr,
):
    s, e, d = lax.axis_index("section"), lax.axis_index("expert"), lax.axis_index("dp")
    h, c = lax.div(d, 2), lax.rem(d, 2)
    other = {"section": s, "expert": e, "dp": h * 2 + (1 - c)}

    def along_z(step):
        z = lax.rem(h * 8 + s + step + 32, 32)
        return {"section": lax.rem(z, 8), "expert": e, "dp": lax.div(z, 8) * 2 + c}

    def plane(i):
        y = lax.rem(lax.div(e, 4) + lax.div(i, 4), 4)
        x = lax.rem(lax.rem(e, 4) + lax.rem(i, 4), 4)
        return y * 4 + x

    def hi(step):
        return lax.rem(h + step, HI)

    saved = [pltpu.make_async_copy(a.at[0, 0], v, load_sem.at[i]) for i, (a, v) in enumerate(((sg, sgv), (su, suv), (gh, ghv)))]
    for copy in saved:
        copy.start()
    weights = []
    for k in range(HI):
        rows = pl.ds(pl.multiple_of(hi(FAR_FIRST[k]) * 2 * BLOCK, 2 * BLOCK), 2 * BLOCK)
        pair = [
            pltpu.make_async_copy(gw.at[0, :, rows], gwv.at[:, rows], w_sem.at[k, 0]),
            pltpu.make_async_copy(uw.at[0, :, rows], uwv.at[:, rows], w_sem.at[k, 1]),
        ]
        for copy in pair:
            copy.start()
        weights.append((rows, pair))

    small = [pltpu.make_async_copy(a.at[0], v, small_sem.at[i]) for i, (a, v) in enumerate(((sec, secv), (rf, rfv), (rb, rbv)))]
    for copy in small:
        copy.start()

    barrier = pltpu.get_barrier_semaphore()

    def greet(i, carry):
        pl.semaphore_signal(barrier, inc=1, device_id={"section": s, "expert": plane(i), "dp": d}, device_id_type=MESH)
        return carry

    for k in range(HI - 1):
        pl.semaphore_signal(
            barrier, inc=1, device_id={"section": s, "expert": e, "dp": hi(FAR_FIRST[k]) * 2 + c}, device_id_type=MESH
        )
    pl.semaphore_signal(barrier, inc=1, device_id=along_z(-1), device_id_type=MESH)
    pl.semaphore_signal(barrier, inc=1, device_id=other, device_id_type=MESH)
    lax.fori_loop(1, EXPERTS, greet, 0)

    for copy in small:
        copy.wait()

    tsend[0:TOK, :] = secv[:, pl.ds(pl.multiple_of(c * HALF, HALF), HALF)]
    tsend[TOK:TOKP, :] = jnp.zeros((TOKP - TOK, HALF), BF16)

    spread = (iota((ROWSP, EXPERTS), 0) // CAPP == iota((ROWSP, EXPERTS), 1)).astype(F32).astype(BF16)
    pos_f, pos_b = positions(rfv[...]), positions(rbv[...])
    within = (iota((ROWSP, TOKP), 0) % CAPP).astype(F32)
    map_f = (dot(spread, pos_f) == within).astype(F32).astype(BF16)
    within_t = (iota((TOKP, ROWSP), 1) % CAPP).astype(F32)
    same = (iota((TOKP, TOKP), 0) == iota((TOKP, TOKP), 1)).astype(F32).astype(BF16)
    pos_b = dot_t(same, pos_b).astype(BF16)
    map_b = (dot_t(pos_b, spread) == within_t).astype(F32).astype(BF16)

    for copy in saved:
        copy.wait()
    g, u, ct = sgv[...].astype(F32), suv[...].astype(F32), ghv[...].astype(F32)
    sig = jax.nn.sigmoid(g)
    grad_up = (ct * g * sig).astype(BF16)
    grad_gate = (ct * u * sig * (1.0 + g * (1.0 - sig))).astype(BF16)
    pad = padding((ROWSP, ROWS), 1)
    grad_up = dot(pad, grad_up).astype(BF16)
    grad_gate = dot(pad, grad_gate).astype(BF16)
    for k in range(HI):
        rows, pair = weights[k]
        for copy in pair:
            copy.wait()
        part = dot(grad_gate, gwv[:, rows]) + dot(grad_up, uwv[:, rows])
        pbuf[k, 0] = part[:, :BLOCK].astype(BF16)
        pbuf[k, 1] = part[:, BLOCK:].astype(BF16)

    pl.semaphore_wait(barrier, EXPERTS - 1 + HI - 1 + 2)

    shift = pltpu.make_async_remote_copy(tsend, trecv, ts, tr, device_id=along_z(1), device_id_type=MESH)
    shift.start()
    swaps = []
    for k in range(HI):
        copy = pltpu.make_async_remote_copy(
            pbuf.at[k, 1 - c], xrecv.at[k], xs.at[k], xr.at[k], device_id=other, device_id_type=MESH
        )
        copy.start()
        swaps.append(copy)

    mine = pl.ds(pl.multiple_of(e * CAPP, CAPP), CAPP)
    for k in range(HI):
        swaps[k].wait_recv()
        asend[k] = (pbuf[k, c].astype(F32) + xrecv[k].astype(F32)).astype(BF16)

        def send(i, carry, k=k):
            to = plane(i)
            pltpu.make_async_remote_copy(
                asend.at[k, pl.ds(pl.multiple_of(to * CAPP, CAPP), CAPP)], arecv.at[k, mine], as_.at[k], ar.at[k],
                device_id={"section": s, "expert": to, "dp": d}, device_id_type=MESH,
            ).start()
            return carry

        lax.fori_loop(1, EXPERTS, send, 0)
        arecv[k, mine] = asend[k, mine]

    shift.wait_recv()
    fsend[...] = dot(map_f, trecv[...]).astype(BF16)
    for p in range(PIECES):
        lanes = pl.ds(p * WIDE, WIDE)

        def send_f(i, carry, p=p, lanes=lanes):
            to = plane(i)
            pltpu.make_async_remote_copy(
                fsend.at[pl.ds(pl.multiple_of(to * CAPP, CAPP), CAPP), lanes], frecv.at[mine, lanes], fs.at[p], fr.at[p],
                device_id={"section": s, "expert": to, "dp": d}, device_id_type=MESH,
            ).start()
            return carry

        lax.fori_loop(1, EXPERTS, send_f, 0)
    frecv[mine, :] = fsend[mine, :]

    most = pl.ds(0, ROWSP - CAPP)
    out_z = []
    own = None
    for k in range(HI):
        pltpu.make_async_copy(asend.at[k, most], arecv.at[k, most], ar.at[k]).wait()
        total = dot(map_b, arecv[k])
        if k == HI - 1:
            own = total.astype(BF16).astype(F32)
            continue
        zsend[k] = total.astype(BF16)
        copy = pltpu.make_async_remote_copy(
            zsend.at[k], zrecv.at[k], zs.at[k], zr.at[k],
            device_id={"section": s, "expert": e, "dp": hi(FAR_FIRST[k]) * 2 + c}, device_id_type=MESH,
        )
        copy.start()
        out_z.append(copy)

    swaps_f = []
    for p in range(PIECES):
        lanes = pl.ds(p * WIDE, WIDE)
        pltpu.make_async_copy(fsend.at[most, lanes], frecv.at[most, lanes], fr.at[p]).wait()
        copy = pltpu.make_async_remote_copy(
            frecv.at[:, lanes], foth.at[:, lanes], gs.at[p], gr.at[p], device_id=other, device_id_type=MESH
        )
        copy.start()
        swaps_f.append(copy)
    near = pl.ds(pl.multiple_of(c * HALF, HALF), HALF)
    far = pl.ds(pl.multiple_of((1 - c) * HALF, HALF), HALF)
    gate = dot_t(frecv[...], gwv[:, near])
    up = dot_t(frecv[...], uwv[:, near])
    for copy in swaps_f:
        copy.wait_recv()
    gate = gate + dot_t(foth[...], gwv[:, far])
    up = up + dot_t(foth[...], uwv[:, far])
    hidden = (gate * jax.nn.sigmoid(gate) * up).astype(BF16)
    hidden_ref[0, 0] = dot(padding((ROWS, ROWSP), 0), hidden).astype(BF16)

    total = own
    for copy in out_z:
        copy.wait_recv()
    for k in range(HI - 1):
        total = total + zrecv[k].astype(F32)
    grad_ref[0] = total[0:TOK].astype(BF16)

    shift.wait_send()
    for copy in (*swaps, *out_z, *swaps_f):
        copy.wait_send()
    for k in range(HI):
        pltpu.make_async_copy(asend.at[k, most], arecv.at[k, most], as_.at[k]).wait()
    for p in range(PIECES):
        lanes = pl.ds(p * WIDE, WIDE)
        pltpu.make_async_copy(fsend.at[most, lanes], frecv.at[most, lanes], fs.at[p]).wait()


def turned(a):
    return jnp.swapaxes(a, 1, 2)


def per_device(section_out, routes_fwd, gate_weight, up_weight, routes_bwd, saved_gate, saved_up, grad_hidden):
    width = gate_weight.shape[2]
    hbm, vmem = pl.BlockSpec(memory_space=pltpu.HBM), pl.BlockSpec(memory_space=pltpu.VMEM)
    dma = pltpu.SemaphoreType.DMA
    return pl.pallas_call(
        kernel,
        out_shape=(
            jax.ShapeDtypeStruct((1, 1, ROWS, width), BF16),
            jax.ShapeDtypeStruct((1, TOK, BLOCK), BF16),
        ),
        in_specs=[hbm] * 8,
        out_specs=(vmem, vmem),
        scratch_shapes=[
            pltpu.VMEM((TOK, D), BF16),
            pltpu.VMEM(routes_fwd.shape[:0:-1], jnp.int32),
            pltpu.VMEM(routes_bwd.shape[:0:-1], jnp.int32),
            pltpu.VMEM((width, D), BF16),
            pltpu.VMEM((width, D), BF16),
            pltpu.VMEM((ROWS, width), BF16),
            pltpu.VMEM((ROWS, width), BF16),
            pltpu.VMEM((ROWS, width), BF16),
            pltpu.VMEM((TOKP, HALF), BF16),
            pltpu.VMEM((TOKP, HALF), BF16),
            pltpu.VMEM((HI, 2, ROWSP, BLOCK), BF16),
            pltpu.VMEM((HI, ROWSP, BLOCK), BF16),
            pltpu.VMEM((HI, ROWSP, BLOCK), BF16),
            pltpu.VMEM((HI, ROWSP, BLOCK), BF16),
            pltpu.VMEM((HI - 1, TOKP, BLOCK), BF16),
            pltpu.VMEM((HI - 1, TOKP, BLOCK), BF16),
            pltpu.VMEM((ROWSP, HALF), BF16),
            pltpu.VMEM((ROWSP, HALF), BF16),
            pltpu.VMEM((ROWSP, HALF), BF16),
            dma((3,)), dma((3,)), dma((HI, 2)), dma, dma, dma((HI,)), dma((HI,)), dma((HI,)), dma((HI,)),
            dma((HI - 1,)), dma((HI - 1,)), dma((PIECES,)), dma((PIECES,)), dma((PIECES,)), dma((PIECES,)),
        ],
        compiler_params=pltpu.CompilerParams(
            collective_id=0, has_side_effects=True, vmem_limit_bytes=60 * 1024 * 1024
        ),
    )(section_out, turned(routes_fwd), turned(gate_weight), turned(up_weight), turned(routes_bwd), saved_gate, saved_up, grad_hidden)


def solution(mesh):
    in_specs = (
        P("section", "expert", None),
        P("section", "expert", None),
        P("expert", None, "dp"),
        P("expert", None, "dp"),
        P("section", "expert", None),
        P("section", "expert", None, "dp"),
        P("section", "expert", None, "dp"),
        P("section", "expert", None, "dp"),
    )
    out_specs = (P("section", "expert", None, "dp"), P("section", "expert", "dp"))
    return jax.shard_map(
        per_device, mesh=mesh, in_specs=in_specs, out_specs=out_specs, check_vma=False
    )
```

time: 152 us -> 62 us (0.41)
  the two profiles are of different devices: /device:TPU:2 before, /device:TPU:1 now
where the time goes in v1:
time: 62 us; the launch traced here: 61.8 us
  Pallas kernels  58.1 us (94%)
  local copies, waits for them, and re-layouts  3.08 us (5%)
  between operations  0.64 us (1%)
    pallas_call x1, Pallas kernels, per_device(): pl.pallas_call(kernel, out_shape=(jax.ShapeDtypeStruct((1, 1, ROWS, width...  58.1 us
    unnamed x2, local copies, waits for them, and re-layouts  3.08 us

profile of v1, /device:TPU:1, one launch (start us, length us, event | category | flops | bytes accessed | tf_op | source)
XLA Modules:
  0.0 61.8 jit_solution(17346346963864366038)
XLA Ops:
  0.6 58.1 %shard_map.95 = (bf16[1,1,208,672]{3,2,1,0:T(8,128)(2,1)}, bf16[1,40,384]{2,1,0:T(8,128)(2,1)}) custom-call(bf16[1,40,3072]{2,1,0:T(8,128)(2,1)} %sec.1, s32[1,4,40]{2,1,0:T(4,128)} %bitcast.6, bf16[1,672,3072]{2,1,0:T(8,128)(2,1)} %bitcast.4, bf16[1,672,3072]{2,1,0:T(8,128)(2,1)} %bitcast.5, s32[1,4,40]{2,1,0:T(4,128)} %bitcast.7, ...), custom_call_target="tpu_custom_call" | custom-call | tf_op jit(solution)/shard_map/pallas_call | solution.py:249
  58.7 1.7 %copy.12 = bf16[1,1,208,672]{3,2,1,0:T(8,128)(2,1)} copy(bf16[1,1,208,672]{3,2,1,0:T(8,128)(2,1)} %get-tuple-element.4) | data formatting | bytes 559104
  60.4 1.4 %copy.13 = bf16[1,40,384]{2,1,0:T(8,128)(2,1)} copy(bf16[1,40,384]{2,1,0:T(8,128)(2,1)} %get-tuple-element.5) | data formatting | bytes 61440

commit v2 on v1

--- a/solution.py
+++ b/solution.py
@@ -55,10 +55,10 @@
 
 def kernel(
     sec, rf, gw, uw, rb, sg, su, gh,
-    hidden_ref, grad_ref,
-    secv, rfv, rbv, gwv, uwv, sgv, suv, ghv,
-    tsend, trecv, pbuf, xrecv, asend, arecv, zsend, zrecv, fsend, frecv, foth,
-    small_sem, load_sem, w_sem, ts, tr, xs, xr, as_, ar, zs, zr, fs, fr, gs, gr,
+    hidden_ref, zrecv,
+    hidv, secv, rfv, rbv, gwv, uwv, sgv, suv, ghv,
+    tsend, trecv, pbuf, xrecv, asend, arecv, zsend, fsend, frecv, foth,
+    out_sem, small_sem, load_sem, w_sem, ts, tr, xs, xr, as_, ar, zs, zr, fs, fr, gs, gr, ready,
 ):
     s, e, d = lax.axis_index("section"), lax.axis_index("expert"), lax.axis_index("dp")
     h, c = lax.div(d, 2), lax.rem(d, 2)
@@ -100,10 +100,12 @@
         pl.semaphore_signal(barrier, inc=1, device_id={"section": s, "expert": plane(i), "dp": d}, device_id_type=MESH)
         return carry
 
-    for k in range(HI - 1):
-        pl.semaphore_signal(
-            barrier, inc=1, device_id={"section": s, "expert": e, "dp": hi(FAR_FIRST[k]) * 2 + c}, device_id_type=MESH
-        )
+    for r in range(1, HI):
+
+        @pl.when(r > h)
+        def _(r=r):
+            pl.semaphore_signal(barrier, inc=1, device_id={"section": s, "expert": e, "dp": r * 2 + c}, device_id_type=MESH)
+
     pl.semaphore_signal(barrier, inc=1, device_id=along_z(-1), device_id_type=MESH)
     pl.semaphore_signal(barrier, inc=1, device_id=other, device_id_type=MESH)
     lax.fori_loop(1, EXPERTS, greet, 0)
@@ -113,15 +115,6 @@
 
     tsend[0:TOK, :] = secv[:, pl.ds(pl.multiple_of(c * HALF, HALF), HALF)]
     tsend[TOK:TOKP, :] = jnp.zeros((TOKP - TOK, HALF), BF16)
-
-    spread = (iota((ROWSP, EXPERTS), 0) // CAPP == iota((ROWSP, EXPERTS), 1)).astype(F32).astype(BF16)
-    pos_f, pos_b = positions(rfv[...]), positions(rbv[...])
-    within = (iota((ROWSP, TOKP), 0) % CAPP).astype(F32)
-    map_f = (dot(spread, pos_f) == within).astype(F32).astype(BF16)
-    within_t = (iota((TOKP, ROWSP), 1) % CAPP).astype(F32)
-    same = (iota((TOKP, TOKP), 0) == iota((TOKP, TOKP), 1)).astype(F32).astype(BF16)
-    pos_b = dot_t(same, pos_b).astype(BF16)
-    map_b = (dot_t(pos_b, spread) == within_t).astype(F32).astype(BF16)
 
     for copy in saved:
         copy.wait()
@@ -132,7 +125,10 @@
     pad = padding((ROWSP, ROWS), 1)
     grad_up = dot(pad, grad_up).astype(BF16)
     grad_gate = dot(pad, grad_gate).astype(BF16)
-    for k in range(HI):
+    mine = pl.ds(pl.multiple_of(e * CAPP, CAPP), CAPP)
+    swaps = []
+
+    def partial(k):
         rows, pair = weights[k]
         for copy in pair:
             copy.wait()
@@ -140,24 +136,18 @@
         pbuf[k, 0] = part[:, :BLOCK].astype(BF16)
         pbuf[k, 1] = part[:, BLOCK:].astype(BF16)
 
-    pl.semaphore_wait(barrier, EXPERTS - 1 + HI - 1 + 2)
-
-    shift = pltpu.make_async_remote_copy(tsend, trecv, ts, tr, device_id=along_z(1), device_id_type=MESH)
-    shift.start()
-    swaps = []
-    for k in range(HI):
+    def swap(k):
         copy = pltpu.make_async_remote_copy(
             pbuf.at[k, 1 - c], xrecv.at[k], xs.at[k], xr.at[k], device_id=other, device_id_type=MESH
         )
         copy.start()
         swaps.append(copy)
 
-    mine = pl.ds(pl.multiple_of(e * CAPP, CAPP), CAPP)
-    for k in range(HI):
+    def spread_out(k):
         swaps[k].wait_recv()
         asend[k] = (pbuf[k, c].astype(F32) + xrecv[k].astype(F32)).astype(BF16)
 
-        def send(i, carry, k=k):
+        def send(i, carry):
             to = plane(i)
             pltpu.make_async_remote_copy(
                 asend.at[k, pl.ds(pl.multiple_of(to * CAPP, CAPP), CAPP)], arecv.at[k, mine], as_.at[k], ar.at[k],
@@ -167,6 +157,66 @@
 
         lax.fori_loop(1, EXPERTS, send, 0)
         arecv[k, mine] = asend[k, mine]
+
+    partial(0)
+    pl.semaphore_wait(barrier, EXPERTS - 1 + 2 + h)
+    shift = pltpu.make_async_remote_copy(tsend, trecv, ts, tr, device_id=along_z(1), device_id_type=MESH)
+    shift.start()
+    swap(0)
+    for r in range(HI - 1):
+
+        @pl.when(r < h)
+        def _(r=r):
+            pl.semaphore_signal(ready, inc=1, device_id={"section": s, "expert": e, "dp": r * 2 + c}, device_id_type=MESH)
+
+    partial(1)
+    swap(1)
+    partial(2)
+    swap(2)
+    spread_out(0)
+    partial(3)
+    swap(3)
+    for k in range(1, HI):
+        spread_out(k)
+
+    spread = (iota((ROWSP, EXPERTS), 0) // CAPP == iota((ROWSP, EXPERTS), 1)).astype(F32).astype(BF16)
+    pos_f, pos_b = positions(rfv[...]), positions(rbv[...])
+    within = (iota((ROWSP, TOKP), 0) % CAPP).astype(F32)
+    map_f = (dot(spread, pos_f) == within).astype(F32).astype(BF16)
+    within_t = (iota((TOKP, ROWSP), 1) % CAPP).astype(F32)
+    same = (iota((TOKP, TOKP), 0) == iota((TOKP, TOKP), 1)).astype(F32).astype(BF16)
+    pos_b = dot_t(same, pos_b).astype(BF16)
+    map_b = (dot_t(pos_b, spread) == within_t).astype(F32).astype(BF16)
+
+    most = pl.ds(0, ROWSP - CAPP)
+    out_z = [
+        pltpu.make_async_remote_copy(
+            zsend.at[k], zrecv.at[k], zs.at[k], zr.at[k],
+            device_id={"section": s, "expert": e, "dp": hi(FAR_FIRST[k]) * 2 + c}, device_id_type=MESH,
+        )
+        for k in range(HI - 1)
+    ]
+
+    def combine(k):
+        pltpu.make_async_copy(asend.at[k, most], arecv.at[k, most], ar.at[k]).wait()
+        zsend[k] = dot(map_b, arecv[k]).astype(BF16)
+
+    @pl.when(h == HI - 2)
+    def _():
+        pl.semaphore_wait(ready, 1)
+
+    @pl.when(h >= 2)
+    def _():
+        for k in range(HI - 1):
+            combine(k)
+            out_z[k].start()
+
+    @pl.when(h < 2)
+    def _():
+        for k in range(HI - 1):
+            combine(k)
+
+    combine(HI - 1)
 
     shift.wait_recv()
     fsend[...] = dot(map_f, trecv[...]).astype(BF16)
@@ -184,22 +234,11 @@
         lax.fori_loop(1, EXPERTS, send_f, 0)
     frecv[mine, :] = fsend[mine, :]
 
-    most = pl.ds(0, ROWSP - CAPP)
-    out_z = []
-    own = None
-    for k in range(HI):
-        pltpu.make_async_copy(asend.at[k, most], arecv.at[k, most], ar.at[k]).wait()
-        total = dot(map_b, arecv[k])
-        if k == HI - 1:
-            own = total.astype(BF16).astype(F32)
-            continue
-        zsend[k] = total.astype(BF16)
-        copy = pltpu.make_async_remote_copy(
-            zsend.at[k], zrecv.at[k], zs.at[k], zr.at[k],
-            device_id={"section": s, "expert": e, "dp": hi(FAR_FIRST[k]) * 2 + c}, device_id_type=MESH,
-        )
-        copy.start()
-        out_z.append(copy)
+    @pl.when(h < 2)
+    def _():
+        pl.semaphore_wait(ready, HI - 1 - h)
+        for k in range(HI - 1):
+            out_z[k].start()
 
     swaps_f = []
     for p in range(PIECES):
@@ -219,15 +258,18 @@
     gate = gate + dot_t(foth[...], gwv[:, far])
     up = up + dot_t(foth[...], uwv[:, far])
     hidden = (gate * jax.nn.sigmoid(gate) * up).astype(BF16)
-    hidden_ref[0, 0] = dot(padding((ROWS, ROWSP), 0), hidden).astype(BF16)
-
-    total = own
+    hidv[...] = dot(padding((ROWS, ROWSP), 0), hidden).astype(BF16)
+    keep = [
+        pltpu.make_async_copy(hidv, hidden_ref, out_sem.at[0]),
+        pltpu.make_async_copy(zsend.at[HI - 1], zrecv.at[HI - 1], out_sem.at[1]),
+    ]
+    for copy in keep:
+        copy.start()
+
+    for copy in keep:
+        copy.wait()
     for copy in out_z:
         copy.wait_recv()
-    for k in range(HI - 1):
-        total = total + zrecv[k].astype(F32)
-    grad_ref[0] = total[0:TOK].astype(BF16)
-
     shift.wait_send()
     for copy in (*swaps, *out_z, *swaps_f):
         copy.wait_send()
@@ -238,23 +280,43 @@
         pltpu.make_async_copy(fsend.at[most, lanes], frecv.at[most, lanes], fs.at[p]).wait()
 
 
+def finish(hidden, blocks, hidden_out, grad_out, hidv, blocksv, gradv, sem):
+    fetch = pltpu.make_async_copy(blocks, blocksv, sem.at[0])
+    fetch.start()
+    bring = pltpu.make_async_copy(hidden, hidv, sem.at[1])
+    bring.start()
+    fetch.wait()
+    total = blocksv[0].astype(F32)
+    for k in range(1, HI):
+        total = total + blocksv[k].astype(F32)
+    gradv[...] = total[0:TOK].astype(BF16)
+    out = pltpu.make_async_copy(gradv, grad_out.at[0], sem.at[2])
+    out.start()
+    bring.wait()
+    put = pltpu.make_async_copy(hidv, hidden_out.at[0, 0], sem.at[3])
+    put.start()
+    out.wait()
+    put.wait()
+
+
 def turned(a):
     return jnp.swapaxes(a, 1, 2)
 
 
 def per_device(section_out, routes_fwd, gate_weight, up_weight, routes_bwd, saved_gate, saved_up, grad_hidden):
     width = gate_weight.shape[2]
-    hbm, vmem = pl.BlockSpec(memory_space=pltpu.HBM), pl.BlockSpec(memory_space=pltpu.VMEM)
+    hbm = pl.BlockSpec(memory_space=pltpu.HBM)
     dma = pltpu.SemaphoreType.DMA
-    return pl.pallas_call(
+    hidden, blocks = pl.pallas_call(
         kernel,
         out_shape=(
-            jax.ShapeDtypeStruct((1, 1, ROWS, width), BF16),
-            jax.ShapeDtypeStruct((1, TOK, BLOCK), BF16),
+            jax.ShapeDtypeStruct((ROWS, width), BF16),
+            jax.ShapeDtypeStruct((HI, TOKP, BLOCK), BF16),
         ),
         in_specs=[hbm] * 8,
-        out_specs=(vmem, vmem),
+        out_specs=(hbm, hbm),
         scratch_shapes=[
+            pltpu.VMEM((ROWS, width), BF16),
             pltpu.VMEM((TOK, D), BF16),
             pltpu.VMEM(routes_fwd.shape[:0:-1], jnp.int32),
             pltpu.VMEM(routes_bwd.shape[:0:-1], jnp.int32),
@@ -269,18 +331,34 @@
             pltpu.VMEM((HI, ROWSP, BLOCK), BF16),
             pltpu.VMEM((HI, ROWSP, BLOCK), BF16),
             pltpu.VMEM((HI, ROWSP, BLOCK), BF16),
-            pltpu.VMEM((HI - 1, TOKP, BLOCK), BF16),
-            pltpu.VMEM((HI - 1, TOKP, BLOCK), BF16),
+            pltpu.VMEM((HI, TOKP, BLOCK), BF16),
             pltpu.VMEM((ROWSP, HALF), BF16),
             pltpu.VMEM((ROWSP, HALF), BF16),
             pltpu.VMEM((ROWSP, HALF), BF16),
-            dma((3,)), dma((3,)), dma((HI, 2)), dma, dma, dma((HI,)), dma((HI,)), dma((HI,)), dma((HI,)),
+            dma((2,)), dma((3,)), dma((3,)), dma((HI, 2)), dma, dma, dma((HI,)), dma((HI,)), dma((HI,)), dma((HI,)),
             dma((HI - 1,)), dma((HI - 1,)), dma((PIECES,)), dma((PIECES,)), dma((PIECES,)), dma((PIECES,)),
+            pltpu.SemaphoreType.REGULAR,
         ],
         compiler_params=pltpu.CompilerParams(
             collective_id=0, has_side_effects=True, vmem_limit_bytes=60 * 1024 * 1024
         ),
     )(section_out, turned(routes_fwd), turned(gate_weight), turned(up_weight), turned(routes_bwd), saved_gate, saved_up, grad_hidden)
+    return pl.pallas_call(
+        finish,
+        out_shape=(
+            jax.ShapeDtypeStruct((1, 1, ROWS, width), BF16),
+            jax.ShapeDtypeStruct((1, TOK, BLOCK), BF16),
+        ),
+        in_specs=[hbm, hbm],
+        out_specs=(hbm, hbm),
+        scratch_shapes=[
+            pltpu.VMEM((ROWS, width), BF16),
+            pltpu.VMEM((HI, TOKP, BLOCK), BF16),
+            pltpu.VMEM((TOK, BLOCK), BF16),
+            dma((4,)),
+        ],
+        compiler_params=pltpu.CompilerParams(vmem_limit_bytes=60 * 1024 * 1024),
+    )(hidden, blocks)
 
 
 def solution(mesh):

time: 62 us -> 54.6 us (0.88)
  Pallas kernels: 58.1 us -> 53.8 us
  local copies, waits for them, and re-layouts: 3.08 us -> 0 us
    pallas_call x1 -> x2, Pallas kernels: 58.1 us -> 53.8 us  [the longest x1 52 us: per_device(): pl.pallas_call(kernel, out_shape=(jax.ShapeDtypeStruct((ROWS, width), BF1...]
    unnamed x2 -> x0, local copies, waits for them, and re-layouts: 3.08 us -> none
where the time goes in v2:
time: 54.6 us; the launch traced here: 54.5 us
  Pallas kernels  53.8 us (99%)
  between operations  0.64 us (1%)
    pallas_call x1, Pallas kernels, per_device(): pl.pallas_call(kernel, out_shape=(jax.ShapeDtypeStruct((ROWS, width), BF1...  52 us
    pallas_call x1, Pallas kernels, per_device(): pl.pallas_call(finish, out_shape=(jax.ShapeDtypeStruct((1, 1, ROWS, width...  1.81 us

profile of v2, /device:TPU:1, one launch (start us, length us, event | category | flops | bytes accessed | tf_op | source)
XLA Modules:
  0.0 54.5 jit_solution(2847790685628358563)
XLA Ops:
  0.6 52.0 %shard_map.95 = (bf16[208,672]{1,0:T(8,128)(2,1)}, bf16[4,48,384]{2,1,0:T(8,128)(2,1)}) custom-call(bf16[1,40,3072]{2,1,0:T(8,128)(2,1)} %sec.1, s32[1,4,40]{2,1,0:T(4,128)} %bitcast.6, bf16[1,672,3072]{2,1,0:T(8,128)(2,1)} %bitcast.4, bf16[1,672,3072]{2,1,0:T(8,128)(2,1)} %bitcast.5, s32[1,4,40]{2,1,0:T(4,128)} %bitcast.7, bf16[1,1,208,672]{3,2,1,0:T(8,128)(2,1)} %sg.1, ...), custom_call_target="tpu_custom_call" | custom-call | tf_op jit(solution)/shard_map/pallas_call | solution.py:310
  52.7 1.8 %shard_map.96 = (bf16[1,1,208,672]{3,2,1,0:T(8,128)(2,1)}, bf16[1,40,384]{2,1,0:T(8,128)(2,1)}) custom-call(bf16[208,672]{1,0:T(8,128)(2,1)} %get-tuple-element.4.hidden, bf16[4,48,384]{2,1,0:T(8,128)(2,1)} %get-tuple-element.5.blocks), custom_call_target="tpu_custom_call" | custom-call | tf_op jit(solution)/shard_map/pallas_call | solution.py:346

commit v3 on v2

--- a/solution.py
+++ b/solution.py
@@ -18,6 +18,9 @@
 D = 3072
 HALF = D // 2
 BLOCK = D // 8
+LANES = 128
+TILES = BLOCK // LANES
+PACK = 128
 HI = 4
 PIECES = 3
 WIDE = HALF // PIECES
@@ -58,7 +61,7 @@
     hidden_ref, zrecv,
     hidv, secv, rfv, rbv, gwv, uwv, sgv, suv, ghv,
     tsend, trecv, pbuf, xrecv, asend, arecv, zsend, fsend, frecv, foth,
-    out_sem, small_sem, load_sem, w_sem, ts, tr, xs, xr, as_, ar, zs, zr, fs, fr, gs, gr, ready,
+    out_sem, small_sem, load_sem, w_sem, ts, tr, xs, xr, as_, ar, zs, zr, fs, fr, gs, gr, ready, follows,
 ):
     s, e, d = lax.axis_index("section"), lax.axis_index("expert"), lax.axis_index("dp")
     h, c = lax.div(d, 2), lax.rem(d, 2)
@@ -75,6 +78,9 @@
 
     def hi(step):
         return lax.rem(h + step, HI)
+
+    def rank(plane_hi):
+        return plane_hi + lax.div(plane_hi, 2) * (5 - 2 * plane_hi)
 
     saved = [pltpu.make_async_copy(a.at[0, 0], v, load_sem.at[i]) for i, (a, v) in enumerate(((sg, sgv), (su, suv), (gh, ghv)))]
     for copy in saved:
@@ -100,13 +106,24 @@
         pl.semaphore_signal(barrier, inc=1, device_id={"section": s, "expert": plane(i), "dp": d}, device_id_type=MESH)
         return carry
 
-    for r in range(1, HI):
-
-        @pl.when(r > h)
-        def _(r=r):
-            pl.semaphore_signal(barrier, inc=1, device_id={"section": s, "expert": e, "dp": r * 2 + c}, device_id_type=MESH)
-
-    pl.semaphore_signal(barrier, inc=1, device_id=along_z(-1), device_id_type=MESH)
+    for step in range(1, HI):
+
+        @pl.when(rank(hi(step)) > rank(h))
+        def _(step=step):
+            to = {"section": s, "expert": e, "dp": hi(step) * 2 + c}
+            pl.semaphore_signal(barrier, inc=1, device_id=to, device_id_type=MESH)
+
+    place = h * 8 + s
+    is_last, is_first = lax.div(place, 31), lax.div(31 - place, 31)
+
+    @pl.when(is_first == 0)
+    def _():
+        pl.semaphore_signal(barrier, inc=1, device_id=along_z(-1), device_id_type=MESH)
+
+    @pl.when(is_last == 1)
+    def _():
+        pl.semaphore_signal(barrier, inc=1, device_id=along_z(1), device_id_type=MESH)
+
     pl.semaphore_signal(barrier, inc=1, device_id=other, device_id_type=MESH)
     lax.fori_loop(1, EXPERTS, greet, 0)
 
@@ -115,6 +132,38 @@
 
     tsend[0:TOK, :] = secv[:, pl.ds(pl.multiple_of(c * HALF, HALF), HALF)]
     tsend[TOK:TOKP, :] = jnp.zeros((TOKP - TOK, HALF), BF16)
+
+    shift = pltpu.make_async_remote_copy(tsend, trecv, ts, tr, device_id=along_z(1), device_id_type=MESH)
+
+    def enter():
+        pl.semaphore_wait(barrier, EXPERTS - 1 + 2 + rank(h) - is_last + is_first)
+
+        @pl.when(is_last == 0)
+        def _():
+            shift.start()
+
+        @pl.when(is_first == 1)
+        def _():
+            pl.semaphore_signal(follows, inc=1, device_id=along_z(-1), device_id_type=MESH)
+
+        for k in range(HI - 1):
+            lower = hi(HI - FAR_FIRST[k])
+
+            @pl.when(rank(lower) < rank(h))
+            def _(k=k, lower=lower):
+                to = {"section": s, "expert": e, "dp": lower * 2 + c}
+                pl.semaphore_signal(ready.at[k], inc=1, device_id=to, device_id_type=MESH)
+
+    enters_late = lax.div(rank(h), HI - 1) + is_last + is_first
+
+    @pl.when(enters_late == 0)
+    def _():
+        enter()
+
+    @pl.when(is_last == 1)
+    def _():
+        pl.semaphore_wait(follows, 1)
+        shift.start()
 
     for copy in saved:
         copy.wait()
@@ -159,21 +208,16 @@
         arecv[k, mine] = asend[k, mine]
 
     partial(0)
-    pl.semaphore_wait(barrier, EXPERTS - 1 + 2 + h)
-    shift = pltpu.make_async_remote_copy(tsend, trecv, ts, tr, device_id=along_z(1), device_id_type=MESH)
-    shift.start()
+    @pl.when(enters_late == 1)
+    def _():
+        enter()
+
     swap(0)
-    for r in range(HI - 1):
-
-        @pl.when(r < h)
-        def _(r=r):
-            pl.semaphore_signal(ready, inc=1, device_id={"section": s, "expert": e, "dp": r * 2 + c}, device_id_type=MESH)
-
     partial(1)
     swap(1)
+    spread_out(0)
     partial(2)
     swap(2)
-    spread_out(0)
     partial(3)
     swap(3)
     for k in range(1, HI):
@@ -188,6 +232,22 @@
     pos_b = dot_t(same, pos_b).astype(BF16)
     map_b = (dot_t(pos_b, spread) == within_t).astype(F32).astype(BF16)
 
+    shift.wait_recv()
+    fsend[...] = dot(map_f, trecv[...]).astype(BF16)
+    for p in range(PIECES):
+        lanes = pl.ds(p * WIDE, WIDE)
+
+        def send_f(i, carry, p=p, lanes=lanes):
+            to = plane(i)
+            pltpu.make_async_remote_copy(
+                fsend.at[pl.ds(pl.multiple_of(to * CAPP, CAPP), CAPP), lanes], frecv.at[mine, lanes], fs.at[p], fr.at[p],
+                device_id={"section": s, "expert": to, "dp": d}, device_id_type=MESH,
+            ).start()
+            return carry
+
+        lax.fori_loop(1, EXPERTS, send_f, 0)
+    frecv[mine, :] = fsend[mine, :]
+
     most = pl.ds(0, ROWSP - CAPP)
     out_z = [
         pltpu.make_async_remote_copy(
@@ -199,45 +259,25 @@
 
     def combine(k):
         pltpu.make_async_copy(asend.at[k, most], arecv.at[k, most], ar.at[k]).wait()
-        zsend[k] = dot(map_b, arecv[k]).astype(BF16)
-
-    @pl.when(h == HI - 2)
-    def _():
-        pl.semaphore_wait(ready, 1)
-
-    @pl.when(h >= 2)
-    def _():
-        for k in range(HI - 1):
-            combine(k)
+        total = dot(map_b, arecv[k])[0:TOK].astype(BF16)
+        for j in range(TILES):
+            zsend[k, j * TOK : (j + 1) * TOK, :] = total[:, j * LANES : (j + 1) * LANES]
+        zsend[k, TILES * TOK : PACK, :] = jnp.zeros((PACK - TILES * TOK, LANES), BF16)
+
+    for k in range(HI - 1):
+        combine(k)
+
+        @pl.when(rank(hi(FAR_FIRST[k])) < rank(h))
+        def _(k=k):
             out_z[k].start()
 
-    @pl.when(h < 2)
-    def _():
-        for k in range(HI - 1):
-            combine(k)
-
     combine(HI - 1)
 
-    shift.wait_recv()
-    fsend[...] = dot(map_f, trecv[...]).astype(BF16)
-    for p in range(PIECES):
-        lanes = pl.ds(p * WIDE, WIDE)
-
-        def send_f(i, carry, p=p, lanes=lanes):
-            to = plane(i)
-            pltpu.make_async_remote_copy(
-                fsend.at[pl.ds(pl.multiple_of(to * CAPP, CAPP), CAPP), lanes], frecv.at[mine, lanes], fs.at[p], fr.at[p],
-                device_id={"section": s, "expert": to, "dp": d}, device_id_type=MESH,
-            ).start()
-            return carry
-
-        lax.fori_loop(1, EXPERTS, send_f, 0)
-    frecv[mine, :] = fsend[mine, :]
-
-    @pl.when(h < 2)
-    def _():
-        pl.semaphore_wait(ready, HI - 1 - h)
-        for k in range(HI - 1):
+    for k in (1, 2, 0):
+
+        @pl.when(rank(hi(FAR_FIRST[k])) > rank(h))
+        def _(k=k):
+            pl.semaphore_wait(ready.at[k], 1)
             out_z[k].start()
 
     swaps_f = []
@@ -289,7 +329,9 @@
     total = blocksv[0].astype(F32)
     for k in range(1, HI):
         total = total + blocksv[k].astype(F32)
-    gradv[...] = total[0:TOK].astype(BF16)
+    total = total.astype(BF16)
+    for j in range(TILES):
+        gradv[:, j * LANES : (j + 1) * LANES] = total[j * TOK : (j + 1) * TOK]
     out = pltpu.make_async_copy(gradv, grad_out.at[0], sem.at[2])
     out.start()
     bring.wait()
@@ -311,7 +353,7 @@
         kernel,
         out_shape=(
             jax.ShapeDtypeStruct((ROWS, width), BF16),
-            jax.ShapeDtypeStruct((HI, TOKP, BLOCK), BF16),
+            jax.ShapeDtypeStruct((HI, PACK, LANES), BF16),
         ),
         in_specs=[hbm] * 8,
         out_specs=(hbm, hbm),
@@ -331,13 +373,13 @@
             pltpu.VMEM((HI, ROWSP, BLOCK), BF16),
             pltpu.VMEM((HI, ROWSP, BLOCK), BF16),
             pltpu.VMEM((HI, ROWSP, BLOCK), BF16),
-            pltpu.VMEM((HI, TOKP, BLOCK), BF16),
+            pltpu.VMEM((HI, PACK, LANES), BF16),
             pltpu.VMEM((ROWSP, HALF), BF16),
             pltpu.VMEM((ROWSP, HALF), BF16),
             pltpu.VMEM((ROWSP, HALF), BF16),
             dma((2,)), dma((3,)), dma((3,)), dma((HI, 2)), dma, dma, dma((HI,)), dma((HI,)), dma((HI,)), dma((HI,)),
             dma((HI - 1,)), dma((HI - 1,)), dma((PIECES,)), dma((PIECES,)), dma((PIECES,)), dma((PIECES,)),
-            pltpu.SemaphoreType.REGULAR,
+            pltpu.SemaphoreType.REGULAR((HI - 1,)), pltpu.SemaphoreType.REGULAR,
         ],
         compiler_params=pltpu.CompilerParams(
             collective_id=0, has_side_effects=True, vmem_limit_bytes=60 * 1024 * 1024
@@ -353,7 +395,7 @@
         out_specs=(hbm, hbm),
         scratch_shapes=[
             pltpu.VMEM((ROWS, width), BF16),
-            pltpu.VMEM((HI, TOKP, BLOCK), BF16),
+            pltpu.VMEM((HI, PACK, LANES), BF16),
             pltpu.VMEM((TOK, BLOCK), BF16),
             dma((4,)),
         ],

time: 54.6 us -> 51.4 us (0.941)
  Pallas kernels: 53.8 us -> 50.6 us
    pallas_call x1, Pallas kernels: 52 us -> 48.8 us  [per_device(): pl.pallas_call(kernel, out_shape=(jax.ShapeDtypeStruct((ROWS, width), BF1...]
where the time goes in v3:
time: 51.4 us; the launch traced here: 51.3 us
  Pallas kernels  50.6 us (98%)
  between operations  0.64 us (1%)
    pallas_call x1, Pallas kernels, per_device(): pl.pallas_call(kernel, out_shape=(jax.ShapeDtypeStruct((ROWS, width), BF1...  48.8 us
    pallas_call x1, Pallas kernels, per_device(): pl.pallas_call(finish, out_shape=(jax.ShapeDtypeStruct((1, 1, ROWS, width...  1.8 us

profile of v3, /device:TPU:1, one launch (start us, length us, event | category | flops | bytes accessed | tf_op | source)
XLA Modules:
  0.0 51.3 jit_solution(8421016241143847774)
XLA Ops:
  0.6 48.8 %shard_map.95 = (bf16[208,672]{1,0:T(8,128)(2,1)}, bf16[4,128,128]{2,1,0:T(8,128)(2,1)}) custom-call(bf16[1,40,3072]{2,1,0:T(8,128)(2,1)} %sec.1, s32[1,4,40]{2,1,0:T(4,128)} %bitcast.6, bf16[1,672,3072]{2,1,0:T(8,128)(2,1)} %bitcast.4, bf16[1,672,3072]{2,1,0:T(8,128)(2,1)} %bitcast.5, s32[1,4,40]{2,1,0:T(4,128)} %bitcast.7, bf16[1,1,208,672]{3,2,1,0:T(8,128)(2,1)} %sg.1, ...), custom_call_target="tpu_custom_call" | custom-call | tf_op jit(solution)/shard_map/pallas_call | solution.py:352
  49.5 1.8 %shard_map.96 = (bf16[1,1,208,672]{3,2,1,0:T(8,128)(2,1)}, bf16[1,40,384]{2,1,0:T(8,128)(2,1)}) custom-call(bf16[208,672]{1,0:T(8,128)(2,1)} %get-tuple-element.4.hidden, bf16[4,128,128]{2,1,0:T(8,128)(2,1)} %get-tuple-element.5.blocks), custom_call_target="tpu_custom_call" | custom-call | tf_op jit(solution)/shard_map/pallas_call | solution.py:388

commit v4 on v3

--- a/solution.py
+++ b/solution.py
@@ -82,6 +82,9 @@
     def rank(plane_hi):
         return plane_hi + lax.div(plane_hi, 2) * (5 - 2 * plane_hi)
 
+    small = [pltpu.make_async_copy(a.at[0], v, small_sem.at[i]) for i, (a, v) in enumerate(((sec, secv), (rf, rfv), (rb, rbv)))]
+    for copy in small:
+        copy.start()
     saved = [pltpu.make_async_copy(a.at[0, 0], v, load_sem.at[i]) for i, (a, v) in enumerate(((sg, sgv), (su, suv), (gh, ghv)))]
     for copy in saved:
         copy.start()
@@ -96,10 +99,6 @@
             copy.start()
         weights.append((rows, pair))
 
-    small = [pltpu.make_async_copy(a.at[0], v, small_sem.at[i]) for i, (a, v) in enumerate(((sec, secv), (rf, rfv), (rb, rbv)))]
-    for copy in small:
-        copy.start()
-
     barrier = pltpu.get_barrier_semaphore()
 
     def greet(i, carry):
@@ -132,6 +131,15 @@
 
     tsend[0:TOK, :] = secv[:, pl.ds(pl.multiple_of(c * HALF, HALF), HALF)]
     tsend[TOK:TOKP, :] = jnp.zeros((TOKP - TOK, HALF), BF16)
+
+    spread = (iota((ROWSP, EXPERTS), 0) // CAPP == iota((ROWSP, EXPERTS), 1)).astype(F32).astype(BF16)
+    pos_f, pos_b = positions(rfv[...]), positions(rbv[...])
+    within = (iota((ROWSP, TOKP), 0) % CAPP).astype(F32)
+    map_f = (dot(spread, pos_f) == within).astype(F32).astype(BF16)
+    within_t = (iota((TOKP, ROWSP), 1) % CAPP).astype(F32)
+    same = (iota((TOKP, TOKP), 0) == iota((TOKP, TOKP), 1)).astype(F32).astype(BF16)
+    pos_b = dot_t(same, pos_b).astype(BF16)
+    map_b = (dot_t(pos_b, spread) == within_t).astype(F32).astype(BF16)
 
     shift = pltpu.make_async_remote_copy(tsend, trecv, ts, tr, device_id=along_z(1), device_id_type=MESH)
 
@@ -222,15 +230,6 @@
     swap(3)
     for k in range(1, HI):
         spread_out(k)
-
-    spread = (iota((ROWSP, EXPERTS), 0) // CAPP == iota((ROWSP, EXPERTS), 1)).astype(F32).astype(BF16)
-    pos_f, pos_b = positions(rfv[...]), positions(rbv[...])
-    within = (iota((ROWSP, TOKP), 0) % CAPP).astype(F32)
-    map_f = (dot(spread, pos_f) == within).astype(F32).astype(BF16)
-    within_t = (iota((TOKP, ROWSP), 1) % CAPP).astype(F32)
-    same = (iota((TOKP, TOKP), 0) == iota((TOKP, TOKP), 1)).astype(F32).astype(BF16)
-    pos_b = dot_t(same, pos_b).astype(BF16)
-    map_b = (dot_t(pos_b, spread) == within_t).astype(F32).astype(BF16)
 
     shift.wait_recv()
     fsend[...] = dot(map_f, trecv[...]).astype(BF16)

time: 51.4 us -> 51.4 us (level)
  no operation moved by 1% of the time
where the time goes in v4:
time: 51.4 us; the launch traced here: 51.3 us
  Pallas kernels  50.6 us (98%)
  between operations  0.64 us (1%)
    pallas_call x1, Pallas kernels, per_device(): pl.pallas_call(kernel, out_shape=(jax.ShapeDtypeStruct((ROWS, width), BF1...  48.8 us
    pallas_call x1, Pallas kernels, per_device(): pl.pallas_call(finish, out_shape=(jax.ShapeDtypeStruct((1, 1, ROWS, width...  1.8 us

profile of v4, /device:TPU:1, one launch (start us, length us, event | category | flops | bytes accessed | tf_op | source)
XLA Modules:
  0.0 51.3 jit_solution(10125873307762297166)
XLA Ops:
  0.6 48.8 %shard_map.95 = (bf16[208,672]{1,0:T(8,128)(2,1)}, bf16[4,128,128]{2,1,0:T(8,128)(2,1)}) custom-call(bf16[1,40,3072]{2,1,0:T(8,128)(2,1)} %sec.1, s32[1,4,40]{2,1,0:T(4,128)} %bitcast.6, bf16[1,672,3072]{2,1,0:T(8,128)(2,1)} %bitcast.4, bf16[1,672,3072]{2,1,0:T(8,128)(2,1)} %bitcast.5, s32[1,4,40]{2,1,0:T(4,128)} %bitcast.7, bf16[1,1,208,672]{3,2,1,0:T(8,128)(2,1)} %sg.1, ...), custom_call_target="tpu_custom_call" | custom-call | tf_op jit(solution)/shard_map/pallas_call | solution.py:351
  49.5 1.8 %shard_map.96 = (bf16[1,1,208,672]{3,2,1,0:T(8,128)(2,1)}, bf16[1,40,384]{2,1,0:T(8,128)(2,1)}) custom-call(bf16[208,672]{1,0:T(8,128)(2,1)} %get-tuple-element.4.hidden, bf16[4,128,128]{2,1,0:T(8,128)(2,1)} %get-tuple-element.5.blocks), custom_call_target="tpu_custom_call" | custom-call | tf_op jit(solution)/shard_map/pallas_call | solution.py:387
